TPU v7x, 256 devices: a whole 4x4x8 slice. The times are simulated.
256 devices in a mesh: grp: 2 (over z_lo), head: 4 (over x), seq: 32 (over y, z_hi, core).
Axes of the slice: x: 4, y: 4, z: 8 (z_hi: 4, z_lo: 2; z = z_hi * 2 + z_lo), core: 2. Of those that a mesh axis runs over, the one named last changes fastest.
Arguments:
- queries: bfloat16 [64, 4096, 128], P('head', 'seq'), may hold values from -6 to 6
- keys: bfloat16 [4, 4096, 128], P('head', 'seq'), may hold values from -6 to 6
- values: bfloat16 [4, 4096, 128], P('head', 'seq'), may hold values from -6 to 6
- feature_map: bfloat16 [64, 128, 128], P('head'), may hold values from -0.5 to 0.5
Outputs:
- feature_grad: float32 [64, 128, 128], P('head', ('grp', 'seq'))
All inputs are finite; a program needn't handle non-finite values.
Results may differ from a plain program's by a relative error of at most 0.0044.
Values may be sent and summed in bfloat16 or wider, within the bound.
A program may use at most 128 MiB of HBM per device.

v0:
```python
import jax
import jax.numpy as jnp
from jax import lax
from jax.sharding import Mesh
from jax.sharding import PartitionSpec as P

SEQ = ("seq_0", "seq_1", "seq_2")
GRP_SEQ = ("grp", "seq_0", "seq_1", "seq_2")


def nothing_yet(value, identity):
    return jax.tree.map(
        lambda a, e: jnp.broadcast_to(jnp.asarray(e, a.dtype), a.shape), value, identity
    )


def prefix_by_axis(value, axes, combine, identity, reverse):
    before = start = nothing_yet(value, identity)
    running = value
    for axis in reversed(axes):
        count, index = (lax.axis_size(axis), lax.axis_index(axis))
        pieces = jax.tree.map(lambda part: lax.all_gather(part, axis), running)
        inside, running = (start, start)
        for k in reversed(range(count)) if reverse else range(count):
            passed = k > index if reverse else k < index
            running = combine(running, jax.tree.map(lambda part: part[k], pieces))
            inside = jax.tree.map(lambda new, old: jnp.where(passed, new, old), running, inside)
        before = combine(inside, before)
    return before


def side_by_side(arrays, axis, dim, along):
    both = jnp.concatenate(arrays, axis=along)
    whole, at, finished = (lax.all_gather(both, axis, axis=dim, tiled=True), 0, [])
    for a in arrays:
        finished.append(lax.slice_in_dim(whole, at, at + a.shape[along], axis=along))
        at += a.shape[along]
    return tuple(finished)


def shifted(value, axis, steps):
    count = lax.axis_size(axis)
    first, last = (max(0, -steps), min(count, count - steps))
    return lax.ppermute(value, axis, [(source, source + steps) for source in range(first, last)])


def split_up(value, dim, count):
    shape = value.shape
    blocks = value.reshape(*shape[:dim], count, shape[dim] // count, *shape[dim + 1 :])
    return jnp.moveaxis(blocks, dim, 0)


def summed_on_arrival(value, axis, dim):
    count = lax.axis_size(axis)
    blocks = lax.all_to_all(split_up(value, dim, count), axis, 0, 0, tiled=True)
    return jnp.sum(blocks, axis=0)


def add_pair(earlier, later):
    return (earlier[0] + later[0], earlier[1] + later[1])


def attend_step(query_rows, own_start):
    scale = 1.0 / jnp.sqrt(jnp.float32(query_rows.shape[-1]))

    def step(carry, pieces, start):
        key_piece, value_piece = pieces
        scores = (
            jnp.einsum("hid,jd->hij", query_rows, key_piece[0], preferred_element_type=jnp.float32)
            * scale
        )
        shape_two = (query_rows.shape[1], key_piece.shape[1])
        row_pos = own_start + lax.broadcasted_iota(jnp.int32, shape_two, 0)
        col_pos = lax.broadcasted_iota(jnp.int32, shape_two, 1)
        weights = jnp.where((col_pos <= row_pos)[None], jnp.exp(scores), jnp.float32(0.0))
        denom = jnp.sum(weights, axis=2)
        numer = jnp.einsum(
            "hij,jd->hid",
            weights.astype(jnp.bfloat16),
            value_piece[0],
            preferred_element_type=jnp.float32,
        )
        return (numer, denom)

    return step


def empty_carry(query_rows):
    return (jnp.zeros(query_rows.shape, jnp.float32), jnp.zeros(query_rows.shape[:2], jnp.float32))


def finish(carry):
    return (carry[0] / carry[1][:, :, None]).astype(jnp.bfloat16)


def student_part(queries, keys, values, feature_map, target, total_tokens, active):
    highest = lax.Precision.HIGHEST
    query_rows = queries.astype(jnp.float32)
    key_rows = keys[0].astype(jnp.float32)
    value_rows = values[0].astype(jnp.float32)
    weights_f = feature_map.astype(jnp.float32)
    tokens_here = key_rows.shape[0]
    lower = jnp.tril(jnp.ones((tokens_here, tokens_here), jnp.float32))
    heads_here = weights_f.shape[0]
    feats = weights_f.shape[2]
    width = value_rows.shape[1]
    zeros_pair = (
        jnp.zeros((heads_here, feats, width), jnp.float32),
        jnp.zeros((heads_here, feats), jnp.float32),
    )

    def key_features(wmat):
        return jnp.exp(jnp.einsum("td,hdf->htf", key_rows, wmat, precision=highest))

    def local_states(wmat):
        phi_k = key_features(wmat)
        return (
            jnp.einsum("htf,td->hfd", phi_k, value_rows, precision=highest),
            jnp.sum(phi_k, axis=1),
        )

    def outputs(wmat, prior, prior_sum):
        phi_q = jnp.exp(jnp.einsum("htd,hdf->htf", query_rows, wmat, precision=highest))
        phi_k = key_features(wmat)
        scores = jnp.einsum("hif,hjf->hij", phi_q, phi_k, precision=highest) * lower[None]
        numer = jnp.einsum("hij,jd->hid", scores, value_rows, precision=highest)
        numer = numer + jnp.einsum("hif,hfd->hid", phi_q, prior, precision=highest)
        denom = jnp.sum(scores, axis=2) + jnp.einsum(
            "hif,hf->hi", phi_q, prior_sum, precision=highest
        )
        return numer / denom[:, :, None]

    states = lax.cond(active, lambda: local_states(weights_f), lambda: zeros_pair)
    prior, prior_sum = prefix_by_axis(states, SEQ, add_pair, zeros_pair, False)

    def backward_outputs():
        student, out_back = jax.vjp(outputs, weights_f, prior, prior_sum)
        cotangent = 2.0 * (student - target.astype(jnp.float32)) / jnp.float32(total_tokens)
        return out_back(cotangent)

    def backward_none():
        return (jnp.zeros_like(weights_f), zeros_pair[0], zeros_pair[1])

    grad_direct, grad_prior, grad_prior_sum = lax.cond(active, backward_outputs, backward_none)
    later = prefix_by_axis((grad_prior, grad_prior_sum), SEQ, add_pair, zeros_pair, True)

    def backward_states():
        state_back = jax.vjp(local_states, weights_f)[1]
        return grad_direct + state_back(later)[0]

    return lax.cond(active, backward_states, lambda: jnp.zeros_like(weights_f))


def per_device(queries, keys, values, feature_map):
    grp_index = lax.axis_index("grp")
    tokens_here = keys.shape[1]
    own_start = lax.axis_index(SEQ) * tokens_here
    total_tokens = tokens_here * lax.axis_size(SEQ)
    is_teacher = grp_index == 0
    inner = attend_step(queries, own_start)
    guarded_carry = empty_carry(queries)
    pieces = side_by_side((keys, values), SEQ, 1, 0)
    start = jnp.int32(0)
    carry = lax.cond(is_teacher, lambda: inner(guarded_carry, pieces, start), lambda: guarded_carry)
    teacher_local = lax.cond(
        is_teacher, lambda: finish(carry), lambda: jnp.zeros(queries.shape, jnp.bfloat16)
    )
    target = shifted(teacher_local, "grp", 1)
    grad_term = student_part(
        queries, keys, values, feature_map, target, total_tokens, grp_index == 1
    )
    return summed_on_arrival(grad_term, GRP_SEQ, 1)


def solution(mesh):
    finer = Mesh(
        mesh.devices.reshape(mesh.shape["grp"], mesh.shape["head"], 4, 4, 2),
        ("grp", "head", "seq_0", "seq_1", "seq_2"),
    )
    placed = (
        P("head", SEQ, None),
        P("head", SEQ, None),
        P("head", SEQ, None),
        P("head", None, None),
    )
    return jax.shard_map(
        per_device, mesh=finer, in_specs=placed, out_specs=P("head", GRP_SEQ, None), check_vma=False
    )
```

profile of v0, /device:TPU:1, one launch (start us, length us, event | category | flops | bytes accessed | tf_op | source)
XLA Modules:
  0.0 477.5 jit_solution(6764870599301474034)
XLA Ops:
  10.0 22.9 %all-gather.22.cloned.1.call-done = f32[32,128,128]{2,1,0:T(8,128)} async-done(((f32[16,128,128]{2,1,0:T(8,128)}), f32[32,128,128]{2,1,0:T(8,128)}) %all-gather.22.cloned.1.call-update) | async-done | bytes 2097168 | tf_op jit(solution)/shard_map/all_gather | solution.py:22
  32.9 2.7 fusion.89
  36.4 77.5 %all-gather.12.cloned.1.call-done = f32[4,16,128,128]{3,2,1,0:T(8,128)} async-done(((f32[1,16,128,128]{3,2,1,0:T(8,128)}), f32[4,16,128,128]{3,2,1,0:T(8,128)}) %all-gather.12.cloned.1.call-update) | async-done | bytes 4194320 | tf_op jit(solution)/shard_map/all_gather | solution.py:22
  113.9 4.7 fusion.94
  120.9 19.1 %all_gather.65 = f32[4,16,128]{2,1,0:T(8,128)S(1)} all-gather(f32[1,16,128]{2,1,0:T(8,128)S(1)} %fusion.87), channel_id=1, replica_groups=mesh['grp'=2,'head'=4,'seq_0'=4,'seq_1'=4,'seq_2'=2] {'seq_1'}, dimensions={0}, use_global_device_ids=true | all-gather | bytes 40960 | tf_op jit(solution)/shard_map/all_gather | solution.py:22
  140.0 9.6 %all_gather.66 = f32[4,16,128]{2,1,0:T(8,128)S(1)} all-gather(f32[1,16,128]{2,1,0:T(8,128)S(1)} %get-tuple-element.1035), channel_id=1, replica_groups=mesh['grp'=2,'head'=4,'seq_0'=4,'seq_1'=4,'seq_2'=2] {'seq_0'}, dimensions={0}, use_global_device_ids=true | all-gather | bytes 40960 | tf_op jit(solution)/shard_map/all_gather | solution.py:22
  149.6 29.3 %all-gather.16.cloned.1.call-done = bf16[2,4096,128]{2,1,0:T(8,128)(2,1)} async-done(((bf16[2,128,128]{2,1,0:T(8,128)(2,1)}), bf16[2,4096,128]{2,1,0:T(8,128)(2,1)}) %all-gather.16.cloned.1.call-update) | async-done | bytes 2097168 | tf_op jit(solution)/shard_map/all_gather | solution.py:34
  178.8 30.8 %conditional.6 = (f32[16,128,128]{2,1,0:T(8,128)S(1)}, f32[16,128]{1,0:T(8,128)S(1)}) conditional(s32[]{:T(128)} %convert_element_type.46, () %tuple.123, (s32[]{:T(128)}, s32[]{:T(128)}, s32[]{:T(128)}, bf16[2,4096,128]{2,1,0:T(8,128)(2,1)}, bf16[16,128,128]{2,1,0:T(8,128)(2,1)S(1)}) %tuple.186), branch_computations={%region_0.0_spmd, %region_1.3_spmd} | conditional | flops 4345821184 | bytes 80749680 | solution.py:164
  179.2 17.1 %fusion = (f32[16,128]{1,0:T(8,128)S(1)}, f32[16,128,4096]{2,1,0:T(8,128)}) fusion(pred[128,4096]{1,0:T(8,128)(4,1)S(1)} %iota_compare_fusion, bf16[16,128,128]{2,1,0:T(8,128)(2,1)S(1)} %get-tuple-element.863, bf16[2,4096,128]{2,1,0:T(8,128)(2,1)} %get-tuple-element.864), kind=kOutput, calls=%fused_computation.1 | convolution fusion | flops 2172647424 | bytes 35659776 | tf_op jit(solution)/shard_map/cond/branch_1_fun/hid,jd->hij/dot_general | solution.py:69
  196.3 13.3 %fusion.2 = f32[16,128,128]{2,1,0:T(8,128)S(1)} fusion(f32[16,128,4096]{2,1,0:T(8,128)} %get-tuple-element.1006, pred[128,4096]{1,0:T(8,128)(4,1)S(1)} %iota_compare_fusion, bf16[2,4096,128]{2,1,0:T(8,128)(2,1)S(1)} %copy-done.8), kind=kOutput, calls=%fused_computation.3 | convolution fusion | flops 2172649472 | bytes 36175872 | tf_op jit(solution)/shard_map/cond/branch_1_fun/hij,jd->hid/dot_general | solution.py:77
  213.5 3.2 slice_bitcast_fusion.2
  216.6 8.2 %collective-permute-done = bf16[16,128,128]{1,2,0:T(8,128)(2,1)S(1)} collective-permute-done((bf16[16,128,128]{1,2,0:T(8,128)(2,1)S(1)}, bf16[16,128,128]{1,2,0:T(8,128)(2,1)S(1)}, u32[]{:S(2)}, u32[]{:S(2)}) %collective-permute-start) | collective-permute-done | bytes 524320 | tf_op jit(solution)/shard_map/ppermute | solution.py:44
  224.8 3.1 all-gather.14.cloned.1.call-done
  229.0 2.2 conditional.8
  231.3 48.5 %all-gather.24.cloned.1.call-done = f32[32,128,128]{2,1,0:T(8,128)} async-done(((f32[16,128,128]{2,1,0:T(8,128)}), f32[32,128,128]{2,1,0:T(8,128)}) %all-gather.24.cloned.1.call-update) | async-done | bytes 2097168 | tf_op jit(solution)/shard_map/all_gather | solution.py:22
  279.7 2.7 fusion.90
  282.5 78.2 %all-gather.18.cloned.1.call-done = f32[4,16,128,128]{3,2,1,0:T(8,128)} async-done(((f32[1,16,128,128]{3,2,1,0:T(8,128)}), f32[4,16,128,128]{3,2,1,0:T(8,128)}) %all-gather.18.cloned.1.call-update) | async-done | bytes 4194320 | tf_op jit(solution)/shard_map/all_gather | solution.py:22
  360.7 4.6 fusion.93
  365.3 2.3 all-gather.2
  367.6 19.1 %all_gather.70 = f32[4,16,128]{2,1,0:T(8,128)S(1)} all-gather(f32[1,16,128]{2,1,0:T(8,128)S(1)} %fusion.88), channel_id=1, replica_groups=mesh['grp'=2,'head'=4,'seq_0'=4,'seq_1'=4,'seq_2'=2] {'seq_1'}, dimensions={0}, use_global_device_ids=true | all-gather | bytes 40960 | tf_op jit(solution)/shard_map/all_gather | solution.py:22
  386.7 10.3 %all_gather.71 = f32[4,16,128]{2,1,0:T(8,128)S(1)} all-gather(f32[1,16,128]{2,1,0:T(8,128)S(1)} %get-tuple-element.1030), channel_id=1, replica_groups=mesh['grp'=2,'head'=4,'seq_0'=4,'seq_1'=4,'seq_2'=2] {'seq_0'}, dimensions={0}, use_global_device_ids=true | all-gather | bytes 40960 | tf_op jit(solution)/shard_map/all_gather | solution.py:22
  397.0 3.2 slice_bitcast_fusion
  400.2 23.4 %all-gather.20.cloned.1.call-done = f32[4,16,128,128]{3,2,1,0:T(8,128)} async-done(((f32[1,16,128,128]{3,2,1,0:T(8,128)}), f32[4,16,128,128]{3,2,1,0:T(8,128)}) %all-gather.20.cloned.1.call-update) | async-done | bytes 4194320 | tf_op jit(solution)/shard_map/all_gather | solution.py:22
  424.2 45.7 %all_to_all.5 = f32[64,16,2,128]{3,1,2,0:T(8,128)S(1)} all-to-all(f32[64,16,2,128]{3,1,2,0:T(8,128)S(1)} %bitcast.389), channel_id=1, replica_groups=mesh['grp'=2,'head'=4,'seq_0'=4,'seq_1'=4,'seq_2'=2] {'grp','seq_0','seq..., dimensions={0} | all-to-all | bytes 2097152 | tf_op jit(solution)/shard_map/all_to_all | solution.py:55
  (59 shorter events, 16.7 us)
Async XLA Ops:
  6.5 26.4 %all-gather.22.cloned.1.call-start = ((), (), s32[]{:S(2)}) async-start(), calls=%async_computation.6 | async-start | bytes 3145728 | tf_op jit(solution)/shard_map/all_gather | solution.py:22
  8.8 26.9 %copy-start.5 = (bf16[1,128,128]{2,1,0:T(8,128)(2,1)S(1)}, bf16[1,128,128]{2,1,0:T(8,128)(2,1)}, u32[]{:S(2)}) copy-start(bf16[1,128,128]{2,1,0:T(8,128)(2,1)} %param.16) | copy-start | bytes 98308
  8.8 26.9 %copy-start.6 = (bf16[1,128,128]{2,1,0:T(8,128)(2,1)S(1)}, bf16[1,128,128]{2,1,0:T(8,128)(2,1)}, u32[]{:S(2)}) copy-start(bf16[1,128,128]{2,1,0:T(8,128)(2,1)} %param.15) | copy-start | bytes 98308
  8.9 1.0 copy-start.3
  9.9 103.9 %all-gather.12.cloned.1.call-start = ((), (), s32[]{:S(2)}) async-start(), calls=%async_computation.1 | async-start | bytes 5242880 | tf_op jit(solution)/shard_map/all_gather | solution.py:22
  35.6 143.2 %all-gather.16.cloned.1.call-start = ((), (), s32[]{:S(2)}) async-start(), calls=%async_computation.3 | async-start | bytes 2162688 | tf_op jit(solution)/shard_map/all_gather | solution.py:34
  36.4 82.3 %copy-start.4 = (bf16[16,128,128]{2,1,0:T(8,128)(2,1)S(1)}, bf16[16,128,128]{2,1,0:T(8,128)(2,1)}, u32[]{:S(2)}) copy-start(bf16[16,128,128]{2,1,0:T(8,128)(2,1)} %param.14) | copy-start | bytes 1572868
  36.4 191.5 %all-gather.14.cloned.1.call-start = ((), (), s32[]{:S(2)}) async-start(), calls=%async_computation.2 | async-start | bytes 5242880 | tf_op jit(solution)/shard_map/all_gather | solution.py:22
  118.6 161.2 %all-gather.24.cloned.1.call-start = ((), (), s32[]{:S(2)}) async-start(), calls=%async_computation.7 | async-start | bytes 3145728 | tf_op jit(solution)/shard_map/all_gather | solution.py:22
  179.2 17.1 %copy-start.8 = (bf16[2,4096,128]{2,1,0:T(8,128)(2,1)S(1)}, bf16[2,4096,128]{2,1,0:T(8,128)(2,1)}, u32[]{:S(2)}) copy-start(bf16[2,4096,128]{2,1,0:T(8,128)(2,1)} %get-tuple-element.864) | copy-start | bytes 6291460 | tf_op jit(solution)/shard_map/cond
  212.1 12.7 %collective-permute-start = (bf16[16,128,128]{1,2,0:T(8,128)(2,1)S(1)}, bf16[16,128,128]{1,2,0:T(8,128)(2,1)S(1)}, u32[]{:S(2)}, u32[]{:S(2)}) collective-permute-start(bf16[16,128,128]{1,2,0:T(8,128)(2,1)S(1)} %copy.52), channel_id=1, source_target_pairs={{0,128},{1,129},{2,130},{3,131},{4,132},{5,133},{6,134},{7,135},{8... | collective-permute-start | bytes 1572872 | tf_op jit(solution)/shard_map/ppermute | solution.py:44
  231.2 129.4 %all-gather.18.cloned.1.call-start = ((), (), s32[]{:S(2)}) async-start(), calls=%async_computation.4 | async-start | bytes 5242880 | tf_op jit(solution)/shard_map/all_gather | solution.py:22
  282.4 141.2 %all-gather.20.cloned.1.call-start = ((), (), s32[]{:S(2)}) async-start(), calls=%async_computation.5 | async-start | bytes 5242880 | tf_op jit(solution)/shard_map/all_gather | solution.py:22
  365.3 58.3 %copy-start.2 = (f32[16,128,128]{2,1,0:T(8,128)S(1)}, f32[16,128,128]{2,1,0:T(8,128)}, u32[]{:S(2)}) copy-start(f32[16,128,128]{2,1,0:T(8,128)} %broadcast.76) | copy-start | bytes 3145732
Sparse Core Ops, SparseCore 0:
  10.0 22.8 all-gather.21
  35.7 78.0 all-gather.11
  116.5 62.2 all-gather.15
  180.5 47.3 all-gather.13
  231.4 48.3 all-gather.23
  282.5 78.0 all-gather.17
  365.4 58.1 all-gather.19
where the time goes:
time: 487 us; the launch traced here: 478 us
  waiting for transfers between devices  291 us (60%)
  blocking collectives  108 us (22%)
  matrix products  30.5 us (6%)
  other arithmetic  17.8 us (4%)
  local copies, waits for them, and re-layouts  14.6 us (3%)
  between operations  13.7 us (3%)
    all_gather x6, waiting for transfers between devices, prefix_by_axis(): pieces = jax.tree.map(lambda part: lax.all_gather(part, axis), running)  254 us
    all_gather x6, blocking collectives, prefix_by_axis(): pieces = jax.tree.map(lambda part: lax.all_gather(part, axis), running)  62.5 us
    all_to_all x1, blocking collectives, summed_on_arrival(): blocks = lax.all_to_all(split_up(value, dim, count), axis, 0, 0, tiled=True)  45.7 us
    all_gather x1, waiting for transfers between devices, side_by_side(): lax.all_gather(both, axis, axis=dim, tiled=True)  29.3 us
    dot_general x1, matrix products, step(): jnp.einsum('hid,jd->hij', query_rows, key_piece[0], preferred_element_typ...  17.1 us
    dot_general x1, matrix products, step(): jnp.einsum('hij,jd->hid', weights.astype(jnp.bfloat16), value_piece[0], p...  13.3 us
  transfers between devices with their start and end apart: 8, of which 8 were waited for; matrix products, arithmetic and copies ran while one was open for 9% of the time, Pallas kernels for 0%

commit v1 on v0

v1 whole, which is shorter than its diff:
```python
import functools
import math

import jax
import jax.numpy as jnp
from jax import lax
from jax.experimental import pallas as pl
from jax.experimental.pallas import tpu as pltpu
from jax.sharding import PartitionSpec as P

MESH = pl.DeviceIdType.MESH
F32 = jnp.float32
BF16 = jnp.bfloat16
BLOCK = 128
CHUNK = 256
D = 128
YS, PAIRS, CORES, GRPS = 4, 4, 2, 2
LAST = (((1,), (1,)), ((), ()))
PLAIN = (((1,), (0,)), ((), ()))


def dot(a, b, dims=PLAIN):
    return lax.dot_general(a, b, dims, preferred_element_type=F32)


def split(x):
    hi = x.astype(BF16)
    return hi, (x - hi.astype(F32)).astype(BF16)


def dot2(a, b, dims=PLAIN):
    return dot(a[0], b, dims) + dot(a[1], b, dims)


def dot3(a, b, dims=PLAIN):
    return dot(a[0], b[0], dims) + (dot(a[0], b[1], dims) + dot(a[1], b[0], dims))


def kernel(
    tokens,
    q_ref,
    k_ref,
    v_ref,
    fm_ref,
    out_ref,
    qbuf,
    kv,
    wbuf,
    phik,
    phiq,
    phiqt,
    intra,
    numer,
    denom,
    state_all,
    state_own,
    cot,
    dphik_own,
    f1_out,
    f1_in,
    f2_out,
    f2_in,
    loc_sem,
    q_send,
    q_recv,
    col_send,
    col_recv,
    right_send,
    right_recv,
    left_send,
    left_recv,
    sib_send,
    sib_recv,
    f1_send,
    f1_recv,
    f2_send,
    f2_recv,
):
    g = lax.axis_index("grp")
    s = lax.axis_index("seq")
    y = lax.div(s, 8)
    zh = lax.rem(lax.div(s, 2), 4)
    c = lax.rem(s, 2)
    z = 2 * zh + g
    head = y * 4 + g * 2 + c

    def seq_of(yy, hh, cc):
        return yy * 8 + hh * 2 + cc

    def device(yy, zz, cc):
        return {"grp": lax.rem(zz, 2), "seq": seq_of(yy, lax.div(zz, 2), cc)}

    def at(zz, yy, cc):
        return kv.at[lax.rem(zz, 2), lax.div(zz, 2), yy, cc]

    def column(zz, cc):
        return kv.at[lax.rem(zz, 2), lax.div(zz, 2), :, cc]

    def remote(src, dst, send, recv, dev):
        return pltpu.make_async_remote_copy(
            src_ref=src, dst_ref=dst, send_sem=send, recv_sem=recv,
            device_id=dev, device_id_type=MESH,
        )

    own = at(z, y, c)

    @pl.when(g == 0)
    def _():
        pltpu.make_async_copy(k_ref.at[0], own, loc_sem.at[0]).start()

    @pl.when(g == 1)
    def _():
        pltpu.make_async_copy(v_ref.at[0], own, loc_sem.at[0]).start()

    copy_q = pltpu.make_async_copy(q_ref.at[head], qbuf.at[y, c], loc_sem.at[1])
    copy_q.start()
    copy_w = pltpu.make_async_copy(fm_ref.at[head], wbuf, loc_sem.at[2])
    copy_w.start()

    other_y = lambda d: lax.rem(y + d, 4)
    other_z = lambda d: lax.rem(z + d, 8)
    other_c = lambda d: lax.rem(c + d, 2)
    group = [
        (dy, dg, dc)
        for dy in range(YS) for dg in range(GRPS) for dc in range(CORES)
        if (dy, dg, dc) != (0, 0, 0)
    ]
    z_pair = lambda d: 2 * zh + lax.rem(g + d, 2)
    next_z, prev_z = other_z(1), other_z(7)
    outer_z = lax.rem(z + 8 + 2 * g - 1, 8)

    barrier = pltpu.get_barrier_semaphore()
    partners = [device(other_y(dy), z_pair(dg), other_c(dc)) for dy, dg, dc in group]
    partners += [device(y, other_z(2 * d), c) for d in (1, 2, 3)]
    partners += [device(y, outer_z, c)]
    for dev in partners:
        pl.semaphore_signal(barrier, inc=1, device_id=dev, device_id_type=MESH)
    pltpu.make_async_copy(k_ref.at[0], own, loc_sem.at[0]).wait()
    pl.semaphore_wait(barrier, len(partners))

    sent = []

    def send(*args):
        copy = remote(*args)
        copy.start()
        sent.append(copy)

    rows = [y, other_y(3), other_y(1), other_y(2)]
    step_of = [0, 1, 3, 2]

    def ring(hop, i):
        if hop < 4 or i < 2:
            ref = at(other_z(8 - (hop - 1)), rows[i], c)
            send(ref, ref, right_send.at[hop - 1, i], right_recv.at[hop - 1, i], device(y, next_z, c))
        if hop < 4 or i >= 2:
            ref = at(other_z(hop - 1), rows[i], c)
            send(ref, ref, left_send.at[hop - 1, i], left_recv.at[hop - 1, i], device(y, prev_z, c))

    def arrived(hop, i):
        if hop < 4 or i < 2:
            ref = at(other_z(8 - hop), rows[i], c)
            remote(ref, ref, right_send.at[hop - 1, i], right_recv.at[hop - 1, i], device(y, prev_z, c)).wait_recv()
        if hop < 4 or i >= 2:
            ref = at(other_z(hop), rows[i], c)
            remote(ref, ref, left_send.at[hop - 1, i], left_recv.at[hop - 1, i], device(y, next_z, c)).wait_recv()

    def sibling(j, offset):
        ref = column(other_z(offset), c)
        send(ref, ref, sib_send.at[j], sib_recv.at[j], device(y, z, other_c(1)))

    def from_sibling(j, offset):
        ref = column(other_z(offset), other_c(1))
        remote(ref, ref, sib_send.at[j], sib_recv.at[j], device(y, z, other_c(1))).wait_recv()

    for i in (1, 2, 3):
        d = step_of[i]
        send(own, own, col_send.at[d], col_recv.at[d], device(other_y(d), z, c))
    ring(1, 0)
    for dy in (1, 3, 2, 0):
        for dc in (0, 1):
            if dy == 0 and dc == 0:
                continue
            to_head = other_y(dy) * 4 + g * 2 + other_c(dc)
            j = dy * 2 + dc
            send(
                q_ref.at[to_head], qbuf.at[y, c], q_send.at[j], q_recv.at[j],
                device(other_y(dy), z, other_c(dc)),
            )

    copy_w.wait()
    w = wbuf[...]
    wt = w.astype(F32).T.astype(BF16)
    ones = jnp.ones((CHUNK, D), BF16)
    row_id = lax.broadcasted_iota(jnp.int32, (CHUNK, CHUNK), 0)
    col_id = lax.broadcasted_iota(jnp.int32, (CHUNK, CHUNK), 1)
    causal = col_id <= row_id
    scale = math.log2(math.e) / math.sqrt(D)

    def query(yq):
        return qbuf[yq].reshape(CHUNK, D)

    def key(pair, yk):
        return kv[0, pair, yk].reshape(CHUNK, D)

    def value(pair, yk):
        return kv[1, pair, yk].reshape(CHUNK, D)

    def value_one(pair, yk):
        return jnp.concatenate([value(pair, yk), ones], axis=1)

    def attend(pair, yq, first, count, masked, new):
        n = count * CHUNK
        keys = kv[0, pair, pl.ds(first, count)].reshape(n, D)
        vals = kv[1, pair, pl.ds(first, count)].reshape(n, D)
        p = jnp.exp2(dot(query(yq), keys, LAST) * scale)
        if masked:
            p = jnp.where(causal, p, 0.0)
        part = sum(p[:, k * D : (k + 1) * D] for k in range(n // D))
        out = dot(p.astype(BF16), vals)
        if new:
            denom[yq] = part
            numer[yq] = out
        else:
            denom[yq] += part
            numer[yq] += out

    def teacher(pair, is_own):
        for yq in range(YS):
            if is_own:
                attend(pair, yq, yq, 1, True, True)
            if yq > 0:
                attend(pair, yq, 0, yq, False, False)
        if not is_own:

            @pl.when(pair < zh)
            def _():
                for yq in range(YS):
                    attend(pair, yq, yq, 1, False, False)

    def student_keys(pair, is_own):
        ks = kv[0, pair].reshape(YS * CHUNK, D)
        phi = jnp.exp(dot(wt, ks, LAST))
        phik[pair] = phi
        for yk in range(YS):
            m = dot(phi[:, yk * CHUNK : (yk + 1) * CHUNK].astype(BF16), value_one(pair, yk))
            if is_own:
                if yk < YS - 1:
                    state_all[yk] = m
                state_own[yk] = jnp.zeros_like(m)
            else:
                if yk < YS - 1:
                    state_all[yk] += m
                state_own[yk] += jnp.where(pair < zh, m, 0.0)

    def student_own():
        for yq in range(YS):
            q = query(yq)
            pq = jnp.exp(dot(q, w))
            phiq[yq] = pq
            phiqt[yq] = jnp.exp(dot(wt, q, LAST))
            pk = phik[zh, :, yq * CHUNK : (yq + 1) * CHUNK]
            scores = jnp.where(causal, dot3(split(pq), split(pk)), 0.0)
            intra[yq] = dot2(split(scores), value_one(zh, yq))

    def work(pair, is_own):
        teacher(pair, is_own)
        student_keys(pair, is_own)

    for i in (1, 2, 3):
        d = step_of[i]
        ref = at(z, rows[i], c)
        remote(ref, ref, col_send.at[d], col_recv.at[d], device(rows[i], z, c)).wait_recv()
        ring(1, i)
    sibling(0, 0)
    for i in range(YS):
        arrived(1, i)
        ring(2, i)
    sibling(1, 7)
    sibling(2, 1)
    copy_q.wait()
    for dy in (1, 3, 2, 0):
        for dc in (0, 1):
            if dy == 0 and dc == 0:
                continue
            j = dy * 2 + dc
            ref = qbuf.at[other_y(4 - dy), other_c(dc)]
            remote(ref, ref, q_send.at[j], q_recv.at[j], device(other_y(4 - dy), z, other_c(dc))).wait_recv()
    from_sibling(0, 0)
    from_sibling(1, 7)
    from_sibling(2, 1)
    near = lax.rem(zh + 2 * g + 3, 4)
    far = lax.rem(zh + 5 - 2 * g, 4)
    opposite = lax.rem(zh + 2, 4)
    work(zh, True)
    for i in range(YS):
        arrived(2, i)
        ring(3, i)
    sibling(3, 6)
    sibling(4, 2)
    student_own()
    from_sibling(3, 6)
    from_sibling(4, 2)
    work(near, False)
    for i in range(YS):
        arrived(3, i)
        ring(4, i)
    sibling(5, 5)
    sibling(6, 3)
    from_sibling(5, 5)
    from_sibling(6, 3)
    work(far, False)
    for i in range(YS):
        arrived(4, i)
    sibling(7, 4)
    from_sibling(7, 4)
    work(opposite, False)

    grad = jnp.zeros((D, D), F32)
    before = None
    for yq in range(YS):
        state = state_own[yq] if before is None else before + state_own[yq]
        if yq < YS - 1:
            before = state_all[yq] if before is None else before + state_all[yq]
        state = state.astype(BF16)
        nd = intra[yq] + dot(phiq[yq].astype(BF16), state)
        inverse = 1.0 / nd[:, D:]
        student = nd[:, :D] * inverse
        total = jnp.sum(denom[yq], axis=1, keepdims=True)
        target = (numer[yq] / total).astype(BF16).astype(F32)
        dn = (student - target) * (2.0 / tokens) * inverse
        dnd = jnp.concatenate([dn, -dn * student], axis=1)
        dnd2 = split(dnd)
        q = query(yq)
        pqt = phiqt[yq]
        pqt2 = split(pqt)
        cot[yq] = dot(pqt2[0], dnd2[0])
        ds = jnp.where(causal, dot2(dnd2, value_one(zh, yq), LAST), 0.0)
        ds2 = split(ds)
        pk2 = split(phik[zh, :, yq * CHUNK : (yq + 1) * CHUNK])
        dpq = dot3(pk2, ds2, LAST) + dot(state, dnd2[0], LAST)
        dphik_own[yq] = dot3(pqt2, ds2)
        grad = grad + dot2(split(pqt * dpq), q)

    for pair, is_own in ((zh, True), (near, False), (far, False), (opposite, False)):
        after = None
        for yk in reversed(range(YS)):
            if is_own:
                gk = after
            else:
                mine = jnp.where(pair < zh, cot[yk], 0.0)
                gk = mine if after is None else after + mine
            after = cot[yk] if after is None else after + cot[yk]
            if gk is None:
                dpk = dphik_own[yk]
            else:
                dpk = dot(gk.astype(BF16), value_one(pair, yk), LAST)
                if is_own:
                    dpk = dpk + dphik_own[yk]
            e = phik[pair, :, yk * CHUNK : (yk + 1) * CHUNK] * dpk
            grad = grad + dot2(split(e), key(pair, yk))

    grad = grad.T
    for hh in range(PAIRS):
        for k in range(8):
            f1_out[hh, k * 4 : k * 4 + 4, :] = grad[k * 16 + hh * 4 : k * 16 + hh * 4 + 4, :]
    for d in (1, 2, 3):
        hh = lax.rem(zh + d, 4)
        send(f1_out.at[hh], f1_in.at[d], f1_send.at[d], f1_recv.at[d], device(y, 2 * hh + g, c))
    acc = f1_out[zh]
    for d in (1, 2, 3):
        hh = lax.rem(zh + 4 - d, 4)
        remote(f1_in.at[d], f1_in.at[d], f1_send.at[d], f1_recv.at[d], device(y, 2 * hh + g, c)).wait_recv()
        acc = acc + f1_in[d]
    for k in range(16):
        f2_out[k] = acc[2 * k : 2 * k + 2, :]
    for j, (dy, dg, dc) in enumerate(group):
        yy, zz, cc = other_y(dy), z_pair(dg), other_c(dc)
        to = lax.rem(zz, 2) * 8 + yy * 2 + cc
        send(f2_out.at[to], f2_in.at[head], f2_send.at[j], f2_recv.at[j], device(yy, zz, cc))
    out_ref[head] = f2_out[g * 8 + y * 2 + c]
    for j, (dy, dg, dc) in enumerate(group):
        yy, zz, cc = other_y(4 - dy), z_pair(dg), other_c(dc)
        source = yy * 4 + lax.rem(zz, 2) * 2 + cc
        ref = f2_in.at[source]
        remote(ref, ref, f2_send.at[j], f2_recv.at[j], device(yy, zz, cc)).wait_recv()
        out_ref[source] = f2_in[source]
    for copy in sent:
        copy.wait_send()


def per_device(queries, keys, values, feature_map):
    heads = queries.shape[0]
    tokens = keys.shape[1] * lax.axis_size("seq")
    dma = pltpu.SemaphoreType.DMA
    anywhere = pl.BlockSpec(memory_space=pl.ANY)
    return pl.pallas_call(
        functools.partial(kernel, tokens),
        out_shape=jax.ShapeDtypeStruct((heads, 2, D), F32),
        in_specs=[anywhere] * 4,
        out_specs=pl.BlockSpec(memory_space=pltpu.VMEM),
        scratch_shapes=[
            pltpu.VMEM((YS, CORES, BLOCK, D), BF16),
            pltpu.VMEM((2, PAIRS, YS, CORES, BLOCK, D), BF16),
            pltpu.VMEM((D, D), BF16),
            pltpu.VMEM((PAIRS, D, YS * CHUNK), F32),
            pltpu.VMEM((YS, CHUNK, D), F32),
            pltpu.VMEM((YS, D, CHUNK), F32),
            pltpu.VMEM((YS, CHUNK, 2 * D), F32),
            pltpu.VMEM((YS, CHUNK, D), F32),
            pltpu.VMEM((YS, CHUNK, D), F32),
            pltpu.VMEM((YS - 1, D, 2 * D), F32),
            pltpu.VMEM((YS, D, 2 * D), F32),
            pltpu.VMEM((YS, D, 2 * D), F32),
            pltpu.VMEM((YS, D, CHUNK), F32),
            pltpu.VMEM((PAIRS, 32, D), F32),
            pltpu.VMEM((PAIRS, 32, D), F32),
            pltpu.VMEM((16, 2, D), F32),
            pltpu.VMEM((16, 2, D), F32),
            dma((3,)),
            dma((8,)),
            dma((8,)),
            dma((4,)),
            dma((4,)),
            dma((4, 4)),
            dma((4, 4)),
            dma((4, 4)),
            dma((4, 4)),
            dma((8,)),
            dma((8,)),
            dma((4,)),
            dma((4,)),
            dma((15,)),
            dma((15,)),
        ],
        compiler_params=pltpu.CompilerParams(
            collective_id=0, has_side_effects=True, vmem_limit_bytes=40 * 2**20
        ),
    )(queries, keys, values, feature_map)


def solution(mesh):
    rows = P("head", "seq", None)
    return jax.shard_map(
        per_device, mesh=mesh, in_specs=(rows, rows, rows, P("head", None, None)),
        out_specs=P("head", ("grp", "seq"), None), check_vma=False,
    )
```

time: 487 us -> 50.3 us (0.10); the launches traced: 478 us -> 50 us
  waiting for transfers between devices: 291 us -> 0 us
  blocking collectives: 108 us -> 0 us
  Pallas kernels: 0 us -> 45.8 us
  matrix products: 30.5 us -> 0 us
  other arithmetic: 17.8 us -> 0 us
  between operations: 13.7 us -> 0.01 us
  local copies, waits for them, and re-layouts: 14.6 us -> 4.2 us
    all_gather x7 -> x0, waiting for transfers between devices: 283 us -> none  [the longest x6 254 us: prefix_by_axis(): pieces = jax.tree.map(lambda part: lax.all_gather(part, axis), running)]
    all_gather x6 -> x0, blocking collectives: 62.5 us -> none  [prefix_by_axis(): pieces = jax.tree.map(lambda part: lax.all_gather(part, axis), running)]
    pallas_call x0 -> x1, Pallas kernels: none -> 45.8 us  [per_device(): pl.pallas_call(functools.partial(kernel, tokens), out_shape=jax.ShapeDtyp...]
    all_to_all x1 -> x0, blocking collectives: 45.7 us -> none  [summed_on_arrival(): blocks = lax.all_to_all(split_up(value, dim, count), axis, 0, 0, tiled=True)]
    dot_general x2 -> x0, matrix products: 30.5 us -> none  [the longest x1 17.1 us: step(): jnp.einsum('hid,jd->hij', query_rows, key_piece[0], preferred_element_typ...]
    slice x4 -> x0, other arithmetic: 9.3 us -> none  [prefix_by_axis(): running = combine(running, jax.tree.map(lambda part: part[k], pieces))]
    ppermute x1 -> x0, waiting for transfers between devices: 8.18 us -> none  [shifted(): lax.ppermute(value, axis, [(source, source + steps) for source in range(f...]
    slice x4 -> x0, local copies, waits for them, and re-layouts: 6.32 us -> none  [prefix_by_axis(): running = combine(running, jax.tree.map(lambda part: part[k], pieces))]
  transfers between devices with their start and end apart: 8 -> 0, of which waited for: 8 -> 0; matrix products, arithmetic and copies ran while one was open for 9% -> 0% of each run, Pallas kernels for 0% -> 0%
where the time goes in v1:
time: 50.3 us; the launch traced here: 50 us
  Pallas kernels  45.8 us (91%)
  local copies, waits for them, and re-layouts  4.2 us (8%)
    pallas_call x1, Pallas kernels, per_device(): pl.pallas_call(functools.partial(kernel, tokens), out_shape=jax.ShapeDtyp...  45.8 us
    unnamed x9, local copies, waits for them, and re-layouts  4.2 us

profile of v1, /device:TPU:1, one launch (start us, length us, event | category | flops | bytes accessed | tf_op | source)
XLA Modules:
  0.0 50.0 jit_solution(13365410849934941649)
XLA Ops:
  0.0 0.0 copy-start
  0.0 1.0 %copy-done = bf16[16,128,128]{2,1,0:T(8,128)(2,1)S(1)} copy-done((bf16[16,128,128]{2,1,0:T(8,128)(2,1)S(1)}, bf16[16,128,128]{2,1,0:T(8,128)(2,1)}, u32[]{:S(2)}) %copy-start) | copy-done | bytes 524312
  1.0 0.0 copy-start.1
  1.0 1.0 %copy-done.1 = bf16[16,128,128]{2,1,0:T(8,128)(2,1)S(1)} copy-done((bf16[16,128,128]{2,1,0:T(8,128)(2,1)S(1)}, bf16[16,128,128]{2,1,0:T(8,128)(2,1)}, u32[]{:S(2)}) %copy-start.1) | copy-done | bytes 524312
  2.1 0.0 copy-start.2
  2.1 0.8 %copy-done.2 = bf16[1,128,128]{2,1,0:T(8,128)(2,1)S(1)} copy-done((bf16[1,128,128]{2,1,0:T(8,128)(2,1)S(1)}, bf16[1,128,128]{2,1,0:T(8,128)(2,1)}, u32[]{:S(2)}) %copy-start.2) | copy-done | bytes 32792
  2.8 0.0 copy-start.3
  2.8 0.8 %copy-done.3 = bf16[1,128,128]{2,1,0:T(8,128)(2,1)S(1)} copy-done((bf16[1,128,128]{2,1,0:T(8,128)(2,1)S(1)}, bf16[1,128,128]{2,1,0:T(8,128)(2,1)}, u32[]{:S(2)}) %copy-start.3) | copy-done | bytes 32792
  3.6 45.8 %shard_map.46 = f32[16,2,128]{2,1,0:T(2,128)S(1)} custom-call(bf16[16,128,128]{2,1,0:T(8,128)(2,1)S(1)} %copy-done, bf16[1,128,128]{2,1,0:T(8,128)(2,1)S(1)} %copy-done.2, bf16[1,128,128]{2,1,0:T(8,128)(2,1)S(1)} %copy-done.3, bf16[16,128,128]{2,1,0:T(8,128)(2,1)S(1)} %copy-done.1), custom_call_target="tpu_custom_call" | custom-call | tf_op jit(solution)/shard_map/pallas_call | solution.py:396
  49.4 0.6 %copy.6 = f32[16,2,128]{2,1,0:T(2,128)} copy(f32[16,2,128]{2,1,0:T(2,128)S(1)} %shard_map.46) | data formatting | bytes 32768
Async XLA Ops:
  0.0 1.0 %copy-start = (bf16[16,128,128]{2,1,0:T(8,128)(2,1)S(1)}, bf16[16,128,128]{2,1,0:T(8,128)(2,1)}, u32[]{:S(2)}) copy-start(bf16[16,128,128]{2,1,0:T(8,128)(2,1)} %q_ref.1) | copy-start | bytes 1572868
  1.0 1.0 %copy-start.1 = (bf16[16,128,128]{2,1,0:T(8,128)(2,1)S(1)}, bf16[16,128,128]{2,1,0:T(8,128)(2,1)}, u32[]{:S(2)}) copy-start(bf16[16,128,128]{2,1,0:T(8,128)(2,1)} %fm_ref.1) | copy-start | bytes 1572868
  2.1 0.8 %copy-start.2 = (bf16[1,128,128]{2,1,0:T(8,128)(2,1)S(1)}, bf16[1,128,128]{2,1,0:T(8,128)(2,1)}, u32[]{:S(2)}) copy-start(bf16[1,128,128]{2,1,0:T(8,128)(2,1)} %k_ref.1) | copy-start | bytes 98308
  2.8 0.8 %copy-start.3 = (bf16[1,128,128]{2,1,0:T(8,128)(2,1)S(1)}, bf16[1,128,128]{2,1,0:T(8,128)(2,1)}, u32[]{:S(2)}) copy-start(bf16[1,128,128]{2,1,0:T(8,128)(2,1)} %v_ref.1) | copy-start | bytes 98308

commit v2 on v1

--- a/solution.py
+++ b/solution.py
@@ -63,12 +63,16 @@
     loc_sem,
     q_send,
     q_recv,
-    col_send,
-    col_recv,
-    right_send,
-    right_recv,
-    left_send,
-    left_recv,
+    z_send,
+    z_recv,
+    up_send,
+    up_recv,
+    down_send,
+    down_recv,
+    key_send,
+    key_recv,
+    value_send,
+    value_recv,
     sib_send,
     sib_recv,
     f1_send,
@@ -90,28 +94,18 @@
     def device(yy, zz, cc):
         return {"grp": lax.rem(zz, 2), "seq": seq_of(yy, lax.div(zz, 2), cc)}
 
-    def at(zz, yy, cc):
-        return kv.at[lax.rem(zz, 2), lax.div(zz, 2), yy, cc]
-
-    def column(zz, cc):
-        return kv.at[lax.rem(zz, 2), lax.div(zz, 2), :, cc]
-
     def remote(src, dst, send, recv, dev):
         return pltpu.make_async_remote_copy(
             src_ref=src, dst_ref=dst, send_sem=send, recv_sem=recv,
             device_id=dev, device_id_type=MESH,
         )
 
-    own = at(z, y, c)
-
-    @pl.when(g == 0)
-    def _():
-        pltpu.make_async_copy(k_ref.at[0], own, loc_sem.at[0]).start()
-
-    @pl.when(g == 1)
-    def _():
-        pltpu.make_async_copy(v_ref.at[0], own, loc_sem.at[0]).start()
-
+    own_copies = [
+        pltpu.make_async_copy(k_ref.at[0], kv.at[0, zh, y, c], loc_sem.at[0]),
+        pltpu.make_async_copy(v_ref.at[0], kv.at[1, zh, y, c], loc_sem.at[3]),
+    ]
+    for copy in own_copies:
+        copy.start()
     copy_q = pltpu.make_async_copy(q_ref.at[head], qbuf.at[y, c], loc_sem.at[1])
     copy_q.start()
     copy_w = pltpu.make_async_copy(fm_ref.at[head], wbuf, loc_sem.at[2])
@@ -126,16 +120,16 @@
         if (dy, dg, dc) != (0, 0, 0)
     ]
     z_pair = lambda d: 2 * zh + lax.rem(g + d, 2)
-    next_z, prev_z = other_z(1), other_z(7)
-    outer_z = lax.rem(z + 8 + 2 * g - 1, 8)
+    toward = lambda d: lax.rem(z + 32 + d * (2 * g - 1), 8)
 
     barrier = pltpu.get_barrier_semaphore()
     partners = [device(other_y(dy), z_pair(dg), other_c(dc)) for dy, dg, dc in group]
     partners += [device(y, other_z(2 * d), c) for d in (1, 2, 3)]
-    partners += [device(y, outer_z, c)]
+    partners += [device(y, toward(d), c) for d in (1, 3)]
     for dev in partners:
         pl.semaphore_signal(barrier, inc=1, device_id=dev, device_id_type=MESH)
-    pltpu.make_async_copy(k_ref.at[0], own, loc_sem.at[0]).wait()
+    for copy in own_copies:
+        copy.wait()
     pl.semaphore_wait(barrier, len(partners))
 
     sent = []
@@ -145,37 +139,48 @@
         copy.start()
         sent.append(copy)
 
-    rows = [y, other_y(3), other_y(1), other_y(2)]
-    step_of = [0, 1, 3, 2]
-
-    def ring(hop, i):
-        if hop < 4 or i < 2:
-            ref = at(other_z(8 - (hop - 1)), rows[i], c)
-            send(ref, ref, right_send.at[hop - 1, i], right_recv.at[hop - 1, i], device(y, next_z, c))
-        if hop < 4 or i >= 2:
-            ref = at(other_z(hop - 1), rows[i], c)
-            send(ref, ref, left_send.at[hop - 1, i], left_recv.at[hop - 1, i], device(y, prev_z, c))
-
-    def arrived(hop, i):
-        if hop < 4 or i < 2:
-            ref = at(other_z(8 - hop), rows[i], c)
-            remote(ref, ref, right_send.at[hop - 1, i], right_recv.at[hop - 1, i], device(y, prev_z, c)).wait_recv()
-        if hop < 4 or i >= 2:
-            ref = at(other_z(hop), rows[i], c)
-            remote(ref, ref, left_send.at[hop - 1, i], left_recv.at[hop - 1, i], device(y, next_z, c)).wait_recv()
-
-    def sibling(j, offset):
-        ref = column(other_z(offset), c)
-        send(ref, ref, sib_send.at[j], sib_recv.at[j], device(y, z, other_c(1)))
-
-    def from_sibling(j, offset):
-        ref = column(other_z(offset), other_c(1))
-        remote(ref, ref, sib_send.at[j], sib_recv.at[j], device(y, z, other_c(1))).wait_recv()
-
-    for i in (1, 2, 3):
-        d = step_of[i]
-        send(own, own, col_send.at[d], col_recv.at[d], device(other_y(d), z, c))
-    ring(1, 0)
+    near = lax.rem(zh + 2 * g + 3, 4)
+    far = lax.rem(zh + 5 - 2 * g, 4)
+    opposite = lax.rem(zh + 2, 4)
+    pairs = [zh, near, far, opposite]
+    up, down, across = other_y(1), other_y(3), other_y(2)
+
+    def block(p, yy):
+        return kv.at[:, pairs[p], yy, c]
+
+    def column(p, cc):
+        return kv.at[:, pairs[p], :, cc]
+
+    def wait_for(ref, send_sem, recv_sem, dev):
+        remote(ref, ref, send_sem, recv_sem, dev).wait_recv()
+
+    def z_arrived(d):
+        source = toward(-2 if d == 2 else d)
+        wait_for(block(d, y), z_send.at[d], z_recv.at[d], device(y, source, c))
+
+    def row_out(p):
+        send(block(p, y), block(p, y), up_send.at[p], up_recv.at[p], device(up, z, c))
+        send(block(p, y), block(p, y), down_send.at[p], down_recv.at[p], device(down, z, c))
+
+    def relay(p):
+        wait_for(block(p, down), up_send.at[p], up_recv.at[p], device(down, z, c))
+        ref = kv.at[0, pairs[p], down, c]
+        send(ref, ref, key_send.at[p], key_recv.at[p], device(up, z, c))
+        wait_for(block(p, up), down_send.at[p], down_recv.at[p], device(up, z, c))
+        ref = kv.at[1, pairs[p], up, c]
+        send(ref, ref, value_send.at[p], value_recv.at[p], device(down, z, c))
+
+    def to_sibling(p):
+        wait_for(kv.at[0, pairs[p], across, c], key_send.at[p], key_recv.at[p], device(down, z, c))
+        wait_for(kv.at[1, pairs[p], across, c], value_send.at[p], value_recv.at[p], device(up, z, c))
+        send(column(p, c), column(p, c), sib_send.at[p], sib_recv.at[p], device(y, z, other_c(1)))
+
+    def from_sibling(p):
+        wait_for(column(p, other_c(1)), sib_send.at[p], sib_recv.at[p], device(y, z, other_c(1)))
+
+    row_out(0)
+    for d in (1, 2, 3):
+        send(block(0, y), block(0, y), z_send.at[d], z_recv.at[d], device(y, toward(d), c))
     for dy in (1, 3, 2, 0):
         for dc in (0, 1):
             if dy == 0 and dc == 0:
@@ -266,17 +271,15 @@
         teacher(pair, is_own)
         student_keys(pair, is_own)
 
-    for i in (1, 2, 3):
-        d = step_of[i]
-        ref = at(z, rows[i], c)
-        remote(ref, ref, col_send.at[d], col_recv.at[d], device(rows[i], z, c)).wait_recv()
-        ring(1, i)
-    sibling(0, 0)
-    for i in range(YS):
-        arrived(1, i)
-        ring(2, i)
-    sibling(1, 7)
-    sibling(2, 1)
+    z_arrived(1)
+    row_out(1)
+    relay(0)
+    z_arrived(2)
+    row_out(2)
+    z_arrived(3)
+    row_out(3)
+    to_sibling(0)
+    relay(1)
     copy_q.wait()
     for dy in (1, 3, 2, 0):
         for dc in (0, 1):
@@ -284,35 +287,20 @@
                 continue
             j = dy * 2 + dc
             ref = qbuf.at[other_y(4 - dy), other_c(dc)]
-            remote(ref, ref, q_send.at[j], q_recv.at[j], device(other_y(4 - dy), z, other_c(dc))).wait_recv()
-    from_sibling(0, 0)
-    from_sibling(1, 7)
-    from_sibling(2, 1)
-    near = lax.rem(zh + 2 * g + 3, 4)
-    far = lax.rem(zh + 5 - 2 * g, 4)
-    opposite = lax.rem(zh + 2, 4)
+            wait_for(ref, q_send.at[j], q_recv.at[j], device(other_y(4 - dy), z, other_c(dc)))
+    from_sibling(0)
     work(zh, True)
-    for i in range(YS):
-        arrived(2, i)
-        ring(3, i)
-    sibling(3, 6)
-    sibling(4, 2)
+    relay(2)
+    to_sibling(1)
     student_own()
-    from_sibling(3, 6)
-    from_sibling(4, 2)
+    from_sibling(1)
     work(near, False)
-    for i in range(YS):
-        arrived(3, i)
-        ring(4, i)
-    sibling(5, 5)
-    sibling(6, 3)
-    from_sibling(5, 5)
-    from_sibling(6, 3)
+    relay(3)
+    to_sibling(2)
+    from_sibling(2)
     work(far, False)
-    for i in range(YS):
-        arrived(4, i)
-    sibling(7, 4)
-    from_sibling(7, 4)
+    to_sibling(3)
+    from_sibling(3)
     work(opposite, False)
 
     grad = jnp.zeros((D, D), F32)
@@ -416,24 +404,28 @@
             pltpu.VMEM((PAIRS, 32, D), F32),
             pltpu.VMEM((16, 2, D), F32),
             pltpu.VMEM((16, 2, D), F32),
-            dma((3,)),
+            dma((4,)),
             dma((8,)),
             dma((8,)),
             dma((4,)),
             dma((4,)),
-            dma((4, 4)),
-            dma((4, 4)),
-            dma((4, 4)),
-            dma((4, 4)),
-            dma((8,)),
-            dma((8,)),
+            dma((4,)),
+            dma((4,)),
+            dma((4,)),
+            dma((4,)),
+            dma((4,)),
+            dma((4,)),
+            dma((4,)),
+            dma((4,)),
+            dma((4,)),
+            dma((4,)),
             dma((4,)),
             dma((4,)),
             dma((15,)),
             dma((15,)),
         ],
         compiler_params=pltpu.CompilerParams(
-            collective_id=0, has_side_effects=True, vmem_limit_bytes=40 * 2**20
+            collective_id=0, has_side_effects=True, vmem_limit_bytes=64 * 2**20 - 2**15
         ),
     )(queries, keys, values, feature_map)
 

time: 50.3 us -> 48.4 us (0.962)
  local copies, waits for them, and re-layouts: 4.2 us -> 1.32 us
  Pallas kernels: 45.8 us -> 46.9 us
    unnamed x9 -> x1, local copies, waits for them, and re-layouts: 4.2 us -> 1.32 us
    pallas_call x1, Pallas kernels: 45.8 us -> 46.9 us  [per_device(): pl.pallas_call(functools.partial(kernel, tokens), out_shape=jax.ShapeDtyp...]
where the time goes in v2:
time: 48.4 us; the launch traced here: 48.3 us
  Pallas kernels  46.9 us (97%)
  local copies, waits for them, and re-layouts  1.32 us (3%)
    pallas_call x1, Pallas kernels, per_device(): pl.pallas_call(functools.partial(kernel, tokens), out_shape=jax.ShapeDtyp...  46.9 us
    unnamed x1, local copies, waits for them, and re-layouts  1.32 us

profile of v2, /device:TPU:1, one launch (start us, length us, event | category | flops | bytes accessed | tf_op | source)
XLA Modules:
  0.0 48.3 jit_solution(8441193075218403458)
XLA Ops:
  0.0 46.9 %shard_map.46 = f32[16,2,128]{2,1,0:T(2,128)} custom-call(bf16[16,128,128]{2,1,0:T(8,128)(2,1)} %q_ref.1, bf16[1,128,128]{2,1,0:T(8,128)(2,1)} %k_ref.1, bf16[1,128,128]{2,1,0:T(8,128)(2,1)} %v_ref.1, bf16[16,128,128]{2,1,0:T(8,128)(2,1)} %fm_ref.1), custom_call_target="tpu_custom_call" | custom-call | tf_op jit(solution)/shard_map/pallas_call | solution.py:384
  46.9 1.3 %copy.6 = f32[16,2,128]{2,1,0:T(2,128)} copy(f32[16,2,128]{2,1,0:T(2,128)} %shard_map.46) | data formatting | bytes 32768

commit v3 on v2

--- a/solution.py
+++ b/solution.py
@@ -65,14 +65,10 @@
     q_recv,
     z_send,
     z_recv,
-    up_send,
-    up_recv,
-    down_send,
-    down_recv,
-    key_send,
-    key_recv,
-    value_send,
-    value_recv,
+    y_send,
+    y_recv,
+    near_send,
+    near_recv,
     sib_send,
     sib_recv,
     f1_send,
@@ -143,44 +139,48 @@
     far = lax.rem(zh + 5 - 2 * g, 4)
     opposite = lax.rem(zh + 2, 4)
     pairs = [zh, near, far, opposite]
-    up, down, across = other_y(1), other_y(3), other_y(2)
 
     def block(p, yy):
         return kv.at[:, pairs[p], yy, c]
 
-    def column(p, cc):
-        return kv.at[:, pairs[p], :, cc]
-
     def wait_for(ref, send_sem, recv_sem, dev):
         remote(ref, ref, send_sem, recv_sem, dev).wait_recv()
+
+    def to_sibling(p, dy):
+        ref = block(p, other_y(dy))
+        send(ref, ref, sib_send.at[p, dy], sib_recv.at[p, dy], device(y, z, other_c(1)))
+
+    def from_sibling(p):
+        for dy in range(YS):
+            ref = kv.at[:, pairs[p], other_y(dy), other_c(1)]
+            wait_for(ref, sib_send.at[p, dy], sib_recv.at[p, dy], device(y, z, other_c(1)))
 
     def z_arrived(d):
         source = toward(-2 if d == 2 else d)
         wait_for(block(d, y), z_send.at[d], z_recv.at[d], device(y, source, c))
+        to_sibling(d, 0)
 
     def row_out(p):
-        send(block(p, y), block(p, y), up_send.at[p], up_recv.at[p], device(up, z, c))
-        send(block(p, y), block(p, y), down_send.at[p], down_recv.at[p], device(down, z, c))
-
-    def relay(p):
-        wait_for(block(p, down), up_send.at[p], up_recv.at[p], device(down, z, c))
-        ref = kv.at[0, pairs[p], down, c]
-        send(ref, ref, key_send.at[p], key_recv.at[p], device(up, z, c))
-        wait_for(block(p, up), down_send.at[p], down_recv.at[p], device(up, z, c))
-        ref = kv.at[1, pairs[p], up, c]
-        send(ref, ref, value_send.at[p], value_recv.at[p], device(down, z, c))
-
-    def to_sibling(p):
-        wait_for(kv.at[0, pairs[p], across, c], key_send.at[p], key_recv.at[p], device(down, z, c))
-        wait_for(kv.at[1, pairs[p], across, c], value_send.at[p], value_recv.at[p], device(up, z, c))
-        send(column(p, c), column(p, c), sib_send.at[p], sib_recv.at[p], device(y, z, other_c(1)))
-
-    def from_sibling(p):
-        wait_for(column(p, other_c(1)), sib_send.at[p], sib_recv.at[p], device(y, z, other_c(1)))
+        for dy in (1, 3, 2):
+            send(block(p, y), block(p, y), y_send.at[p, dy], y_recv.at[p, dy], device(other_y(dy), z, c))
+
+    def rows_in(p):
+        for dy in (1, 3, 2):
+            ref = block(p, other_y(4 - dy))
+            wait_for(ref, y_send.at[p, dy], y_recv.at[p, dy], device(other_y(4 - dy), z, c))
+            if p == 0:
+                send(ref, ref, near_send.at[4 - dy], near_recv.at[4 - dy], device(y, toward(1), c))
+            to_sibling(p, 4 - dy)
+
+    def near_in():
+        for dy in (3, 1, 2):
+            wait_for(block(1, other_y(dy)), near_send.at[dy], near_recv.at[dy], device(y, toward(1), c))
+            to_sibling(1, dy)
 
     row_out(0)
     for d in (1, 2, 3):
         send(block(0, y), block(0, y), z_send.at[d], z_recv.at[d], device(y, toward(d), c))
+    to_sibling(0, 0)
     for dy in (1, 3, 2, 0):
         for dc in (0, 1):
             if dy == 0 and dc == 0:
@@ -272,14 +272,11 @@
         student_keys(pair, is_own)
 
     z_arrived(1)
-    row_out(1)
-    relay(0)
+    rows_in(0)
     z_arrived(2)
     row_out(2)
     z_arrived(3)
     row_out(3)
-    to_sibling(0)
-    relay(1)
     copy_q.wait()
     for dy in (1, 3, 2, 0):
         for dc in (0, 1):
@@ -290,16 +287,14 @@
             wait_for(ref, q_send.at[j], q_recv.at[j], device(other_y(4 - dy), z, other_c(dc)))
     from_sibling(0)
     work(zh, True)
-    relay(2)
-    to_sibling(1)
+    near_in()
     student_own()
+    rows_in(2)
     from_sibling(1)
     work(near, False)
-    relay(3)
-    to_sibling(2)
+    rows_in(3)
     from_sibling(2)
     work(far, False)
-    to_sibling(3)
     from_sibling(3)
     work(opposite, False)
 
@@ -409,16 +404,12 @@
             dma((8,)),
             dma((4,)),
             dma((4,)),
-            dma((4,)),
-            dma((4,)),
-            dma((4,)),
-            dma((4,)),
-            dma((4,)),
-            dma((4,)),
-            dma((4,)),
-            dma((4,)),
-            dma((4,)),
-            dma((4,)),
+            dma((4, 4)),
+            dma((4, 4)),
+            dma((4,)),
+            dma((4,)),
+            dma((4, 4)),
+            dma((4, 4)),
             dma((4,)),
             dma((4,)),
             dma((15,)),

time: 48.4 us -> 45.2 us (0.934)
  Pallas kernels: 46.9 us -> 43.7 us
    pallas_call x1, Pallas kernels: 46.9 us -> 43.7 us  [per_device(): pl.pallas_call(functools.partial(kernel, tokens), out_shape=jax.ShapeDtyp...]
where the time goes in v3:
time: 45.2 us; the launch traced here: 45.1 us
  Pallas kernels  43.7 us (97%)
  local copies, waits for them, and re-layouts  1.32 us (3%)
    pallas_call x1, Pallas kernels, per_device(): pl.pallas_call(functools.partial(kernel, tokens), out_shape=jax.ShapeDtyp...  43.7 us
    unnamed x1, local copies, waits for them, and re-layouts  1.32 us

profile of v3, /device:TPU:1, one launch (start us, length us, event | category | flops | bytes accessed | tf_op | source)
XLA Modules:
  0.0 45.1 jit_solution(15111784535312087457)
XLA Ops:
  0.0 43.7 %shard_map.46 = f32[16,2,128]{2,1,0:T(2,128)} custom-call(bf16[16,128,128]{2,1,0:T(8,128)(2,1)} %q_ref.1, bf16[1,128,128]{2,1,0:T(8,128)(2,1)} %k_ref.1, bf16[1,128,128]{2,1,0:T(8,128)(2,1)} %v_ref.1, bf16[16,128,128]{2,1,0:T(8,128)(2,1)} %fm_ref.1), custom_call_target="tpu_custom_call" | custom-call | tf_op jit(solution)/shard_map/pallas_call | solution.py:379
  43.7 1.3 %copy.6 = f32[16,2,128]{2,1,0:T(2,128)} copy(f32[16,2,128]{2,1,0:T(2,128)} %shard_map.46) | data formatting | bytes 32768

commit v4 on v3

--- a/solution.py
+++ b/solution.py
@@ -29,11 +29,13 @@
 
 
 def dot2(a, b, dims=PLAIN):
-    return dot(a[0], b, dims) + dot(a[1], b, dims)
+    rows = a[0].shape[0]
+    both = dot(jnp.concatenate(a, axis=0), b, dims)
+    return both[:rows] + both[rows:]
 
 
 def dot3(a, b, dims=PLAIN):
-    return dot(a[0], b[0], dims) + (dot(a[0], b[1], dims) + dot(a[1], b[0], dims))
+    return dot2(a, b[0], dims) + dot(a[0], b[1], dims)
 
 
 def kernel(
@@ -54,8 +56,6 @@
     denom,
     state_all,
     state_own,
-    cot,
-    dphik_own,
     f1_out,
     f1_in,
     f2_out,
@@ -213,34 +213,22 @@
     def value_one(pair, yk):
         return jnp.concatenate([value(pair, yk), ones], axis=1)
 
-    def attend(pair, yq, first, count, masked, new):
-        n = count * CHUNK
-        keys = kv[0, pair, pl.ds(first, count)].reshape(n, D)
-        vals = kv[1, pair, pl.ds(first, count)].reshape(n, D)
-        p = jnp.exp2(dot(query(yq), keys, LAST) * scale)
-        if masked:
-            p = jnp.where(causal, p, 0.0)
-        part = sum(p[:, k * D : (k + 1) * D] for k in range(n // D))
-        out = dot(p.astype(BF16), vals)
-        if new:
-            denom[yq] = part
-            numer[yq] = out
-        else:
-            denom[yq] += part
-            numer[yq] += out
-
     def teacher(pair, is_own):
         for yq in range(YS):
+            n = (yq + 1) * CHUNK
+            keys = kv[0, pair, 0 : yq + 1].reshape(n, D)
+            vals = kv[1, pair, 0 : yq + 1].reshape(n, D)
+            p = jnp.exp2(dot(query(yq), keys, LAST) * scale)
+            last = jnp.where(causal if is_own else pair < zh, p[:, n - CHUNK :], 0.0)
+            p = jnp.concatenate([p[:, : n - CHUNK], last], axis=1) if yq else last
+            part = sum(p[:, k * D : (k + 1) * D] for k in range(n // D))
+            out = dot(p.astype(BF16), vals)
             if is_own:
-                attend(pair, yq, yq, 1, True, True)
-            if yq > 0:
-                attend(pair, yq, 0, yq, False, False)
-        if not is_own:
-
-            @pl.when(pair < zh)
-            def _():
-                for yq in range(YS):
-                    attend(pair, yq, yq, 1, False, False)
+                denom[yq] = part
+                numer[yq] = out
+            else:
+                denom[yq] += part
+                numer[yq] += out
 
     def student_keys(pair, is_own):
         ks = kv[0, pair].reshape(YS * CHUNK, D)
@@ -298,49 +286,52 @@
     from_sibling(3)
     work(opposite, False)
 
-    grad = jnp.zeros((D, D), F32)
-    before = None
-    for yq in range(YS):
+    chunks = range(YS)
+    qs = [query(yq) for yq in chunks]
+    vones = [value_one(zh, yq) for yq in chunks]
+    states, before = [], None
+    for yq in chunks:
         state = state_own[yq] if before is None else before + state_own[yq]
         if yq < YS - 1:
             before = state_all[yq] if before is None else before + state_all[yq]
-        state = state.astype(BF16)
-        nd = intra[yq] + dot(phiq[yq].astype(BF16), state)
-        inverse = 1.0 / nd[:, D:]
-        student = nd[:, :D] * inverse
+        states.append(state.astype(BF16))
+    outs = [intra[yq] + dot(phiq[yq].astype(BF16), states[yq]) for yq in chunks]
+    dnds = []
+    for yq in chunks:
+        inverse = 1.0 / outs[yq][:, D:]
+        student = outs[yq][:, :D] * inverse
         total = jnp.sum(denom[yq], axis=1, keepdims=True)
         target = (numer[yq] / total).astype(BF16).astype(F32)
         dn = (student - target) * (2.0 / tokens) * inverse
-        dnd = jnp.concatenate([dn, -dn * student], axis=1)
-        dnd2 = split(dnd)
-        q = query(yq)
-        pqt = phiqt[yq]
-        pqt2 = split(pqt)
-        cot[yq] = dot(pqt2[0], dnd2[0])
-        ds = jnp.where(causal, dot2(dnd2, value_one(zh, yq), LAST), 0.0)
-        ds2 = split(ds)
-        pk2 = split(phik[zh, :, yq * CHUNK : (yq + 1) * CHUNK])
-        dpq = dot3(pk2, ds2, LAST) + dot(state, dnd2[0], LAST)
-        dphik_own[yq] = dot3(pqt2, ds2)
-        grad = grad + dot2(split(pqt * dpq), q)
-
-    for pair, is_own in ((zh, True), (near, False), (far, False), (opposite, False)):
-        after = None
-        for yk in reversed(range(YS)):
-            if is_own:
-                gk = after
-            else:
-                mine = jnp.where(pair < zh, cot[yk], 0.0)
-                gk = mine if after is None else after + mine
-            after = cot[yk] if after is None else after + cot[yk]
-            if gk is None:
-                dpk = dphik_own[yk]
-            else:
-                dpk = dot(gk.astype(BF16), value_one(pair, yk), LAST)
-                if is_own:
-                    dpk = dpk + dphik_own[yk]
-            e = phik[pair, :, yk * CHUNK : (yk + 1) * CHUNK] * dpk
-            grad = grad + dot2(split(e), key(pair, yk))
+        dnds.append(split(jnp.concatenate([dn, -dn * student], axis=1)))
+    pqts = [split(phiqt[yq]) for yq in chunks]
+    pks = [split(phik[zh, :, yq * CHUNK : (yq + 1) * CHUNK]) for yq in chunks]
+    cots = [dot(pqts[yq][0], dnds[yq][0]) for yq in chunks]
+    dss = [
+        split(jnp.where(causal, dot2(dnds[yq], vones[yq], LAST), 0.0)) for yq in chunks
+    ]
+    dpqs = [dot3(pks[yq], dss[yq], LAST) + dot(states[yq], dnds[yq][0], LAST) for yq in chunks]
+    dpks_own = [dot3(pqts[yq], dss[yq]) for yq in chunks]
+    later = [None] * YS
+    for yk in reversed(range(YS - 1)):
+        later[yk] = cots[yk + 1] if later[yk + 1] is None else later[yk + 1] + cots[yk + 1]
+    grad = jnp.zeros((D, D), F32)
+    for pair, is_own in ((near, False), (far, False), (opposite, False), (zh, True)):
+        dpks = []
+        for yk in chunks:
+            gk = later[yk]
+            if not is_own:
+                mine = jnp.where(pair < zh, cots[yk], 0.0)
+                gk = mine if gk is None else gk + mine
+            dpk = dpks_own[yk] if is_own else None
+            if gk is not None:
+                far_part = dot(gk.astype(BF16), value_one(pair, yk), LAST)
+                dpk = far_part if dpk is None else dpk + far_part
+            dpks.append(dpk)
+        e = phik[pair] * jnp.concatenate(dpks, axis=1)
+        grad = grad + dot2(split(e), kv[0, pair].reshape(YS * CHUNK, D))
+    e = jnp.concatenate([phiqt[yq] * dpqs[yq] for yq in chunks], axis=1)
+    grad = grad + dot2(split(e), qbuf[...].reshape(YS * CHUNK, D))
 
     grad = grad.T
     for hh in range(PAIRS):
@@ -393,8 +384,6 @@
             pltpu.VMEM((YS, CHUNK, D), F32),
             pltpu.VMEM((YS - 1, D, 2 * D), F32),
             pltpu.VMEM((YS, D, 2 * D), F32),
-            pltpu.VMEM((YS, D, 2 * D), F32),
-            pltpu.VMEM((YS, D, CHUNK), F32),
             pltpu.VMEM((PAIRS, 32, D), F32),
             pltpu.VMEM((PAIRS, 32, D), F32),
             pltpu.VMEM((16, 2, D), F32),

time: 45.2 us -> 42.2 us (0.934)
  Pallas kernels: 43.7 us -> 40.7 us
    pallas_call x1, Pallas kernels: 43.7 us -> 40.7 us  [per_device(): pl.pallas_call(functools.partial(kernel, tokens), out_shape=jax.ShapeDtyp...]
where the time goes in v4:
time: 42.2 us; the launch traced here: 42 us
  Pallas kernels  40.7 us (96%)
  local copies, waits for them, and re-layouts  1.32 us (3%)
    pallas_call x1, Pallas kernels, per_device(): pl.pallas_call(functools.partial(kernel, tokens), out_shape=jax.ShapeDtyp...  40.7 us
    unnamed x1, local copies, waits for them, and re-layouts  1.32 us

profile of v4, /device:TPU:1, one launch (start us, length us, event | category | flops | bytes accessed | tf_op | source)
XLA Modules:
  0.0 42.0 jit_solution(3533515098302163657)
XLA Ops:
  0.0 40.7 %shard_map.46 = f32[16,2,128]{2,1,0:T(2,128)} custom-call(bf16[16,128,128]{2,1,0:T(8,128)(2,1)} %q_ref.1, bf16[1,128,128]{2,1,0:T(8,128)(2,1)} %k_ref.1, bf16[1,128,128]{2,1,0:T(8,128)(2,1)} %v_ref.1, bf16[16,128,128]{2,1,0:T(8,128)(2,1)} %fm_ref.1), custom_call_target="tpu_custom_call" | custom-call | tf_op jit(solution)/shard_map/pallas_call | solution.py:370
  40.7 1.3 %copy.6 = f32[16,2,128]{2,1,0:T(2,128)} copy(f32[16,2,128]{2,1,0:T(2,128)} %shard_map.46) | data formatting | bytes 32768

commit v5 on v4

--- a/solution.py
+++ b/solution.py
@@ -108,7 +108,6 @@
     copy_w.start()
 
     other_y = lambda d: lax.rem(y + d, 4)
-    other_z = lambda d: lax.rem(z + d, 8)
     other_c = lambda d: lax.rem(c + d, 2)
     group = [
         (dy, dg, dc)
@@ -119,9 +118,8 @@
     toward = lambda d: lax.rem(z + 32 + d * (2 * g - 1), 8)
 
     barrier = pltpu.get_barrier_semaphore()
-    partners = [device(other_y(dy), z_pair(dg), other_c(dc)) for dy, dg, dc in group]
-    partners += [device(y, other_z(2 * d), c) for d in (1, 2, 3)]
-    partners += [device(y, toward(d), c) for d in (1, 3)]
+    partners = [device(y, toward(d), c) for d in (3, 2, 1, -2)]
+    partners += [device(other_y(dy), z, other_c(dc)) for dy, dg, dc in group if dg == 0]
     for dev in partners:
         pl.semaphore_signal(barrier, inc=1, device_id=dev, device_id_type=MESH)
     for copy in own_copies:
@@ -214,21 +212,20 @@
         return jnp.concatenate([value(pair, yk), ones], axis=1)
 
     def teacher(pair, is_own):
-        for yq in range(YS):
-            n = (yq + 1) * CHUNK
-            keys = kv[0, pair, 0 : yq + 1].reshape(n, D)
-            vals = kv[1, pair, 0 : yq + 1].reshape(n, D)
-            p = jnp.exp2(dot(query(yq), keys, LAST) * scale)
-            last = jnp.where(causal if is_own else pair < zh, p[:, n - CHUNK :], 0.0)
-            p = jnp.concatenate([p[:, : n - CHUNK], last], axis=1) if yq else last
-            part = sum(p[:, k * D : (k + 1) * D] for k in range(n // D))
-            out = dot(p.astype(BF16), vals)
-            if is_own:
-                denom[yq] = part
-                numer[yq] = out
+        for yk in range(YS):
+            queries = qbuf[yk:].reshape((YS - yk) * CHUNK, D)
+            p = jnp.exp2(dot(queries, key(pair, yk), LAST) * scale)
+            first = jnp.where(causal if is_own else pair < zh, p[:CHUNK], 0.0)
+            p = jnp.concatenate([first, p[CHUNK:]], axis=0) if yk < YS - 1 else first
+            part = p[:, :D] + p[:, D:]
+            out = dot(p.astype(BF16), value(pair, yk))
+            rows = pl.ds(yk * CHUNK, (YS - yk) * CHUNK)
+            if is_own and yk == 0:
+                denom[rows] = part
+                numer[rows] = out
             else:
-                denom[yq] += part
-                numer[yq] += out
+                denom[rows] += part
+                numer[rows] += out
 
     def student_keys(pair, is_own):
         ks = kv[0, pair].reshape(YS * CHUNK, D)
@@ -300,8 +297,9 @@
     for yq in chunks:
         inverse = 1.0 / outs[yq][:, D:]
         student = outs[yq][:, :D] * inverse
-        total = jnp.sum(denom[yq], axis=1, keepdims=True)
-        target = (numer[yq] / total).astype(BF16).astype(F32)
+        rows = pl.ds(yq * CHUNK, CHUNK)
+        total = jnp.sum(denom[rows], axis=1, keepdims=True)
+        target = (numer[rows] / total).astype(BF16).astype(F32)
         dn = (student - target) * (2.0 / tokens) * inverse
         dnds.append(split(jnp.concatenate([dn, -dn * student], axis=1)))
     pqts = [split(phiqt[yq]) for yq in chunks]
@@ -337,7 +335,7 @@
     for hh in range(PAIRS):
         for k in range(8):
             f1_out[hh, k * 4 : k * 4 + 4, :] = grad[k * 16 + hh * 4 : k * 16 + hh * 4 + 4, :]
-    for d in (1, 2, 3):
+    for d in (2, 1, 3):
         hh = lax.rem(zh + d, 4)
         send(f1_out.at[hh], f1_in.at[d], f1_send.at[d], f1_recv.at[d], device(y, 2 * hh + g, c))
     acc = f1_out[zh]
@@ -380,8 +378,8 @@
             pltpu.VMEM((YS, CHUNK, D), F32),
             pltpu.VMEM((YS, D, CHUNK), F32),
             pltpu.VMEM((YS, CHUNK, 2 * D), F32),
-            pltpu.VMEM((YS, CHUNK, D), F32),
-            pltpu.VMEM((YS, CHUNK, D), F32),
+            pltpu.VMEM((YS * CHUNK, D), F32),
+            pltpu.VMEM((YS * CHUNK, D), F32),
             pltpu.VMEM((YS - 1, D, 2 * D), F32),
             pltpu.VMEM((YS, D, 2 * D), F32),
             pltpu.VMEM((PAIRS, 32, D), F32),

time: 42.2 us -> 41.1 us (0.974)
  Pallas kernels: 40.7 us -> 39.5 us
    pallas_call x1, Pallas kernels: 40.7 us -> 39.5 us  [per_device(): pl.pallas_call(functools.partial(kernel, tokens), out_shape=jax.ShapeDtyp...]
where the time goes in v5:
time: 41.1 us; the launch traced here: 40.9 us
  Pallas kernels  39.5 us (96%)
  local copies, waits for them, and re-layouts  1.32 us (3%)
    pallas_call x1, Pallas kernels, per_device(): pl.pallas_call(functools.partial(kernel, tokens), out_shape=jax.ShapeDtyp...  39.5 us
    unnamed x1, local copies, waits for them, and re-layouts  1.32 us

profile of v5, /device:TPU:1, one launch (start us, length us, event | category | flops | bytes accessed | tf_op | source)
XLA Modules:
  0.0 40.9 jit_solution(2529505830896952376)
XLA Ops:
  0.0 39.5 %shard_map.46 = f32[16,2,128]{2,1,0:T(2,128)} custom-call(bf16[16,128,128]{2,1,0:T(8,128)(2,1)} %q_ref.1, bf16[1,128,128]{2,1,0:T(8,128)(2,1)} %k_ref.1, bf16[1,128,128]{2,1,0:T(8,128)(2,1)} %v_ref.1, bf16[16,128,128]{2,1,0:T(8,128)(2,1)} %fm_ref.1), custom_call_target="tpu_custom_call" | custom-call | tf_op jit(solution)/shard_map/pallas_call | solution.py:368
  39.6 1.3 %copy.6 = f32[16,2,128]{2,1,0:T(2,128)} copy(f32[16,2,128]{2,1,0:T(2,128)} %shard_map.46) | data formatting | bytes 32768

commit v6 on v5

--- a/solution.py
+++ b/solution.py
@@ -133,6 +133,11 @@
         copy.start()
         sent.append(copy)
 
+    def settle(count):
+        for copy in sent[:count]:
+            copy.wait_send()
+        del sent[:count]
+
     near = lax.rem(zh + 2 * g + 3, 4)
     far = lax.rem(zh + 5 - 2 * g, 4)
     opposite = lax.rem(zh + 2, 4)
@@ -285,7 +290,7 @@
 
     chunks = range(YS)
     qs = [query(yq) for yq in chunks]
-    vones = [value_one(zh, yq) for yq in chunks]
+    twice = [jnp.concatenate([value(zh, yq)] * 2, axis=1) for yq in chunks]
     states, before = [], None
     for yq in chunks:
         state = state_own[yq] if before is None else before + state_own[yq]
@@ -293,7 +298,7 @@
             before = state_all[yq] if before is None else before + state_all[yq]
         states.append(state.astype(BF16))
     outs = [intra[yq] + dot(phiq[yq].astype(BF16), states[yq]) for yq in chunks]
-    dnds = []
+    dnds, dns, dds = [], [], []
     for yq in chunks:
         inverse = 1.0 / outs[yq][:, D:]
         student = outs[yq][:, :D] * inverse
@@ -301,29 +306,34 @@
         total = jnp.sum(denom[rows], axis=1, keepdims=True)
         target = (numer[rows] / total).astype(BF16).astype(F32)
         dn = (student - target) * (2.0 / tokens) * inverse
-        dnds.append(split(jnp.concatenate([dn, -dn * student], axis=1)))
+        dd = -dn * student
+        dnds.append(jnp.concatenate([dn, dd], axis=1).astype(BF16))
+        dns.append(jnp.concatenate(split(dn), axis=1))
+        dds.append(jnp.sum(dd, axis=1, keepdims=True))
     pqts = [split(phiqt[yq]) for yq in chunks]
     pks = [split(phik[zh, :, yq * CHUNK : (yq + 1) * CHUNK]) for yq in chunks]
-    cots = [dot(pqts[yq][0], dnds[yq][0]) for yq in chunks]
+    cots = [dot(pqts[yq][0], dnds[yq]) for yq in chunks]
     dss = [
-        split(jnp.where(causal, dot2(dnds[yq], vones[yq], LAST), 0.0)) for yq in chunks
+        split(jnp.where(causal, dot(dns[yq], twice[yq], LAST) + dds[yq], 0.0)) for yq in chunks
     ]
-    dpqs = [dot3(pks[yq], dss[yq], LAST) + dot(states[yq], dnds[yq][0], LAST) for yq in chunks]
+    dpqs = [dot3(pks[yq], dss[yq], LAST) + dot(states[yq], dnds[yq], LAST) for yq in chunks]
     dpks_own = [dot3(pqts[yq], dss[yq]) for yq in chunks]
+    cots = [(m[:, :D], jnp.sum(m[:, D:], axis=1, keepdims=True)) for m in cots]
+    add = lambda a, b: (a[0] + b[0], a[1] + b[1])
     later = [None] * YS
     for yk in reversed(range(YS - 1)):
-        later[yk] = cots[yk + 1] if later[yk + 1] is None else later[yk + 1] + cots[yk + 1]
+        later[yk] = cots[yk + 1] if later[yk + 1] is None else add(later[yk + 1], cots[yk + 1])
     grad = jnp.zeros((D, D), F32)
     for pair, is_own in ((near, False), (far, False), (opposite, False), (zh, True)):
         dpks = []
         for yk in chunks:
             gk = later[yk]
             if not is_own:
-                mine = jnp.where(pair < zh, cots[yk], 0.0)
-                gk = mine if gk is None else gk + mine
+                mine = tuple(jnp.where(pair < zh, part, 0.0) for part in cots[yk])
+                gk = mine if gk is None else add(gk, mine)
             dpk = dpks_own[yk] if is_own else None
             if gk is not None:
-                far_part = dot(gk.astype(BF16), value_one(pair, yk), LAST)
+                far_part = dot(gk[0].astype(BF16), value(pair, yk), LAST) + gk[1]
                 dpk = far_part if dpk is None else dpk + far_part
             dpks.append(dpk)
         e = phik[pair] * jnp.concatenate(dpks, axis=1)
@@ -338,6 +348,7 @@
     for d in (2, 1, 3):
         hh = lax.rem(zh + d, 4)
         send(f1_out.at[hh], f1_in.at[d], f1_send.at[d], f1_recv.at[d], device(y, 2 * hh + g, c))
+    settle(len(sent) - 3)
     acc = f1_out[zh]
     for d in (1, 2, 3):
         hh = lax.rem(zh + 4 - d, 4)
@@ -349,6 +360,7 @@
         yy, zz, cc = other_y(dy), z_pair(dg), other_c(dc)
         to = lax.rem(zz, 2) * 8 + yy * 2 + cc
         send(f2_out.at[to], f2_in.at[head], f2_send.at[j], f2_recv.at[j], device(yy, zz, cc))
+    settle(3)
     out_ref[head] = f2_out[g * 8 + y * 2 + c]
     for j, (dy, dg, dc) in enumerate(group):
         yy, zz, cc = other_y(4 - dy), z_pair(dg), other_c(dc)
@@ -356,8 +368,7 @@
         ref = f2_in.at[source]
         remote(ref, ref, f2_send.at[j], f2_recv.at[j], device(yy, zz, cc)).wait_recv()
         out_ref[source] = f2_in[source]
-    for copy in sent:
-        copy.wait_send()
+    settle(len(sent))
 
 
 def per_device(queries, keys, values, feature_map):

time: 41.1 us -> 40.8 us (level)
  no operation moved by 1% of the time
where the time goes in v6:
time: 40.8 us; the launch traced here: 40.6 us
  Pallas kernels  39.3 us (96%)
  local copies, waits for them, and re-layouts  1.32 us (3%)
    pallas_call x1, Pallas kernels, per_device(): pl.pallas_call(functools.partial(kernel, tokens), out_shape=jax.ShapeDtyp...  39.3 us
    unnamed x1, local copies, waits for them, and re-layouts  1.32 us

profile of v6, /device:TPU:1, one launch (start us, length us, event | category | flops | bytes accessed | tf_op | source)
XLA Modules:
  0.0 40.6 jit_solution(1901772602836468321)
XLA Ops:
  0.0 39.3 %shard_map.46 = f32[16,2,128]{2,1,0:T(2,128)} custom-call(bf16[16,128,128]{2,1,0:T(8,128)(2,1)} %q_ref.1, bf16[1,128,128]{2,1,0:T(8,128)(2,1)} %k_ref.1, bf16[1,128,128]{2,1,0:T(8,128)(2,1)} %v_ref.1, bf16[16,128,128]{2,1,0:T(8,128)(2,1)} %fm_ref.1), custom_call_target="tpu_custom_call" | custom-call | tf_op jit(solution)/shard_map/pallas_call | solution.py:379
  39.3 1.3 %copy.6 = f32[16,2,128]{2,1,0:T(2,128)} copy(f32[16,2,128]{2,1,0:T(2,128)} %shard_map.46) | data formatting | bytes 32768

commit v7 on v6

--- a/solution.py
+++ b/solution.py
@@ -14,7 +14,7 @@
 BLOCK = 128
 CHUNK = 256
 D = 128
-YS, PAIRS, CORES, GRPS = 4, 4, 2, 2
+YS, PAIRS, CORES = 4, 4, 2
 LAST = (((1,), (1,)), ((), ()))
 PLAIN = (((1,), (0,)), ((), ()))
 
@@ -111,7 +111,7 @@
     other_c = lambda d: lax.rem(c + d, 2)
     group = [
         (dy, dg, dc)
-        for dy in range(YS) for dg in range(GRPS) for dc in range(CORES)
+        for dy in (2, 1, 3, 0) for dg in (1, 0) for dc in (1, 0)
         if (dy, dg, dc) != (0, 0, 0)
     ]
     z_pair = lambda d: 2 * zh + lax.rem(g + d, 2)
@@ -216,14 +216,20 @@
     def value_one(pair, yk):
         return jnp.concatenate([value(pair, yk), ones], axis=1)
 
-    def teacher(pair, is_own):
+    def teacher(group, is_own):
         for yk in range(YS):
             queries = qbuf[yk:].reshape((YS - yk) * CHUNK, D)
-            p = jnp.exp2(dot(queries, key(pair, yk), LAST) * scale)
-            first = jnp.where(causal if is_own else pair < zh, p[:CHUNK], 0.0)
+            keys = jnp.concatenate([key(pair, yk) for pair in group], axis=0)
+            vals = jnp.concatenate([value(pair, yk) for pair in group], axis=0)
+            p = jnp.exp2(dot(queries, keys, LAST) * scale)
+            first = [
+                jnp.where(causal if is_own else pair < zh, p[:CHUNK, k * CHUNK : (k + 1) * CHUNK], 0.0)
+                for k, pair in enumerate(group)
+            ]
+            first = jnp.concatenate(first, axis=1)
             p = jnp.concatenate([first, p[CHUNK:]], axis=0) if yk < YS - 1 else first
-            part = p[:, :D] + p[:, D:]
-            out = dot(p.astype(BF16), value(pair, yk))
+            part = sum(p[:, k * D : (k + 1) * D] for k in range(2 * len(group)))
+            out = dot(p.astype(BF16), vals)
             rows = pl.ds(yk * CHUNK, (YS - yk) * CHUNK)
             if is_own and yk == 0:
                 denom[rows] = part
@@ -257,9 +263,10 @@
             scores = jnp.where(causal, dot3(split(pq), split(pk)), 0.0)
             intra[yq] = dot2(split(scores), value_one(zh, yq))
 
-    def work(pair, is_own):
-        teacher(pair, is_own)
-        student_keys(pair, is_own)
+    def work(group, is_own):
+        teacher(group, is_own)
+        for pair in group:
+            student_keys(pair, is_own)
 
     z_arrived(1)
     rows_in(0)
@@ -276,17 +283,18 @@
             ref = qbuf.at[other_y(4 - dy), other_c(dc)]
             wait_for(ref, q_send.at[j], q_recv.at[j], device(other_y(4 - dy), z, other_c(dc)))
     from_sibling(0)
-    work(zh, True)
+    work([zh], True)
     near_in()
     student_own()
     rows_in(2)
     from_sibling(1)
-    work(near, False)
+    student_keys(near, False)
     rows_in(3)
     from_sibling(2)
-    work(far, False)
+    student_keys(far, False)
     from_sibling(3)
-    work(opposite, False)
+    teacher([near, far, opposite], False)
+    student_keys(opposite, False)
 
     chunks = range(YS)
     qs = [query(yq) for yq in chunks]

time: 40.8 us -> 40.3 us (0.988)
  Pallas kernels: 39.3 us -> 38.8 us
    pallas_call x1, Pallas kernels: 39.3 us -> 38.8 us  [per_device(): pl.pallas_call(functools.partial(kernel, tokens), out_shape=jax.ShapeDtyp...]
where the time goes in v7:
time: 40.3 us; the launch traced here: 40.1 us
  Pallas kernels  38.8 us (96%)
  local copies, waits for them, and re-layouts  1.32 us (3%)
    pallas_call x1, Pallas kernels, per_device(): pl.pallas_call(functools.partial(kernel, tokens), out_shape=jax.ShapeDtyp...  38.8 us
    unnamed x1, local copies, waits for them, and re-layouts  1.32 us

profile of v7, /device:TPU:1, one launch (start us, length us, event | category | flops | bytes accessed | tf_op | source)
XLA Modules:
  0.0 40.1 jit_solution(10989580662583506998)
XLA Ops:
  0.0 38.8 %shard_map.46 = f32[16,2,128]{2,1,0:T(2,128)} custom-call(bf16[16,128,128]{2,1,0:T(8,128)(2,1)} %q_ref.1, bf16[1,128,128]{2,1,0:T(8,128)(2,1)} %k_ref.1, bf16[1,128,128]{2,1,0:T(8,128)(2,1)} %v_ref.1, bf16[16,128,128]{2,1,0:T(8,128)(2,1)} %fm_ref.1), custom_call_target="tpu_custom_call" | custom-call | tf_op jit(solution)/shard_map/pallas_call | solution.py:387
  38.8 1.3 %copy.6 = f32[16,2,128]{2,1,0:T(2,128)} copy(f32[16,2,128]{2,1,0:T(2,128)} %shard_map.46) | data formatting | bytes 32768

commit v8 on v7

--- a/solution.py
+++ b/solution.py
@@ -367,15 +367,12 @@
     for j, (dy, dg, dc) in enumerate(group):
         yy, zz, cc = other_y(dy), z_pair(dg), other_c(dc)
         to = lax.rem(zz, 2) * 8 + yy * 2 + cc
-        send(f2_out.at[to], f2_in.at[head], f2_send.at[j], f2_recv.at[j], device(yy, zz, cc))
+        send(f2_out.at[to], f2_in.at[head], f2_send.at[j], f2_recv.at[0], device(yy, zz, cc))
     settle(3)
-    out_ref[head] = f2_out[g * 8 + y * 2 + c]
-    for j, (dy, dg, dc) in enumerate(group):
-        yy, zz, cc = other_y(4 - dy), z_pair(dg), other_c(dc)
-        source = yy * 4 + lax.rem(zz, 2) * 2 + cc
-        ref = f2_in.at[source]
-        remote(ref, ref, f2_send.at[j], f2_recv.at[j], device(yy, zz, cc)).wait_recv()
-        out_ref[source] = f2_in[source]
+    f2_in[head] = f2_out[g * 8 + y * 2 + c]
+    every = f2_in.at[pl.ds(0, len(group))]
+    wait_for(every, f2_send.at[0], f2_recv.at[0], partners[-1])
+    out_ref[...] = f2_in[...]
     settle(len(sent))
 
 

time: 40.3 us -> 40.3 us (level)
  no operation moved by 1% of the time
where the time goes in v8:
time: 40.3 us; the launch traced here: 40.1 us
  Pallas kernels  38.7 us (96%)
  local copies, waits for them, and re-layouts  1.32 us (3%)
    pallas_call x1, Pallas kernels, per_device(): pl.pallas_call(functools.partial(kernel, tokens), out_shape=jax.ShapeDtyp...  38.7 us
    unnamed x1, local copies, waits for them, and re-layouts  1.32 us

profile of v8, /device:TPU:1, one launch (start us, length us, event | category | flops | bytes accessed | tf_op | source)
XLA Modules:
  0.0 40.1 jit_solution(11772883804934349320)
XLA Ops:
  0.0 38.7 %shard_map.46 = f32[16,2,128]{2,1,0:T(2,128)} custom-call(bf16[16,128,128]{2,1,0:T(8,128)(2,1)} %q_ref.1, bf16[1,128,128]{2,1,0:T(8,128)(2,1)} %k_ref.1, bf16[1,128,128]{2,1,0:T(8,128)(2,1)} %v_ref.1, bf16[16,128,128]{2,1,0:T(8,128)(2,1)} %fm_ref.1), custom_call_target="tpu_custom_call" | custom-call | tf_op jit(solution)/shard_map/pallas_call | solution.py:384
  38.7 1.3 %copy.6 = f32[16,2,128]{2,1,0:T(2,128)} copy(f32[16,2,128]{2,1,0:T(2,128)} %shard_map.46) | data formatting | bytes 32768
